TPU v7x, 32 devices: a whole 2x2x4 slice. The times are simulated.
32 devices in a mesh: freq: 8 (over y, x, core), node: 4 (over z).
Axes of the slice: x: 2, y: 2, z: 4, core: 2. Of those that a mesh axis runs over, the one named last changes fastest.
Arguments:
- pressure: bfloat16 [2, 128, 4, 8192], P(None, 'freq', None, 'node'), may hold values from -6 to 6
- spectrum_amp: float32 [4, 128], replicated, may hold values from 0.03 to 0.3
- phase_code: int32 [4, 128], replicated, may hold values from 0 to 4095
- panel_tile: int32 [8, 4, 256, 1], P('freq'), may hold values from 0 to 63; in each aligned block of 1024 rows (0 to 1023, 1024 to 2047, ..., all dimensions but the last counted through in order) at most 24 rows name the same one
- patch_weight: bfloat16 [8, 4, 256, 128], P('freq'), may hold values from 0 to 0.099609375
Outputs:
- node_loads: bfloat16 [4, 4096, 8192], P(None, 'node', 'freq')
Inputs may be any that keep to these rules, and one draw needn't show every extreme that they name: Within each block panel_tile[g] (1024 panels), no patch is named by more than 24 panels, a bound that some block reaches; every patch is named somewhere.
All inputs are finite; a program needn't handle non-finite values.
Results may differ from a plain program's by a relative error of at most 0.0062.
Values may be sent and summed in bfloat16 or wider, within the bound.
A program may use at most 128 MiB of HBM per device.

v0:
```python
import math

import jax
import jax.numpy as jnp
from jax import lax
from jax.sharding import PartitionSpec as P

F = 128
TSTEPS = 4096
BIN_STEP = 15
PHASE_LEVELS = 4096
TILE_DEV = 8


def scale_spectra(pressure, spectrum_amp, phase_code):
    phase_angle = phase_code.astype(jnp.float32) * (2.0 * math.pi / PHASE_LEVELS)
    amplitude = spectrum_amp.T[:, :, None]
    cosine = jnp.cos(phase_angle).T[:, :, None]
    sine_part = jnp.sin(phase_angle).T[:, :, None]
    real_part = pressure[0].astype(jnp.float32)
    imag_part = pressure[1].astype(jnp.float32)
    scaled_re = amplitude * (real_part * cosine - imag_part * sine_part)
    scaled_im = amplitude * (real_part * sine_part + imag_part * cosine)
    return jnp.stack([scaled_re, scaled_im]).astype(jnp.bfloat16)


def basis_table(first_step, step_count):
    freq_bin = 1 + BIN_STEP * jnp.arange(F, dtype=jnp.int32)
    step_ids = first_step + jnp.arange(step_count, dtype=jnp.int32)
    turn_count = freq_bin[:, None] * step_ids[None, :] % TSTEPS
    turn_angle = turn_count.astype(jnp.float32) * (2.0 * math.pi / TSTEPS)
    return jnp.concatenate([jnp.cos(turn_angle), -jnp.sin(turn_angle)], axis=0).astype(jnp.bfloat16)


def slot_members(tile_ids, tile_count, capacity):
    row_count = tile_ids.shape[0]
    onehot = (tile_ids[:, None] == jnp.arange(tile_count, dtype=jnp.int32)[None, :]).astype(
        jnp.int32
    )
    slot_rank = jnp.sum((jnp.cumsum(onehot, axis=0) - onehot) * onehot, axis=1)
    slot_index = tile_ids * capacity + slot_rank
    empty = jnp.full((tile_count * capacity,), row_count, jnp.int32)
    return empty.at[slot_index].set(jnp.arange(row_count, dtype=jnp.int32))


def shards(pressure, spectrum_amp, phase_code, panel_tile, patch_weight):
    regrouped = lax.all_to_all(pressure, "freq", split_axis=3, concat_axis=1, tiled=True)
    scaled = scale_spectra(regrouped, spectrum_amp, phase_code)
    freq_count = scaled.shape[1]
    headings = scaled.shape[2]
    panels = scaled.shape[3]
    owners = lax.axis_size("freq")
    windows = lax.axis_size("node")
    window_len = TSTEPS // windows
    first_step = lax.axis_index("node") * window_len
    tile_count = owners * TILE_DEV
    capacity = max(2, 3 * windows * panels // (2 * TILE_DEV * owners))
    tile_ids = panel_tile.reshape(-1)
    weights = patch_weight.reshape(-1, 128)
    members = slot_members(tile_ids, tile_count, capacity)
    sent_weight = jnp.take(weights, members, axis=0, mode="fill", fill_value=0)
    sent_weight = sent_weight.reshape(1, owners, TILE_DEV, capacity, 128)
    spectra = lax.all_gather(scaled, "node", axis=3, tiled=True)
    sent_spectra = jnp.take(spectra, members, axis=3, mode="fill", fill_value=0)
    sent_spectra = sent_spectra.reshape(2 * freq_count * headings, owners, TILE_DEV, capacity)
    wave_basis = basis_table(first_step, window_len)
    got_spectra = lax.all_to_all(sent_spectra, "freq", split_axis=1, concat_axis=1, tiled=True)
    got_weight = lax.all_to_all(sent_weight, "freq", split_axis=1, concat_axis=1, tiled=True)
    shaped = got_spectra.reshape((2 * freq_count, headings) + got_spectra.shape[1:])
    series = jnp.einsum(
        "qhskc,qt->hskct", shaped, wave_basis, preferred_element_type=jnp.float32
    ).astype(jnp.bfloat16)
    partial_value = jnp.einsum(
        "hskct,skcn->htkn", series, got_weight[0], preferred_element_type=jnp.float32
    )
    node_loads = partial_value.reshape(partial_value.shape[0], partial_value.shape[1], -1)
    return node_loads.astype(jnp.bfloat16)


def solution(mesh):
    placed = (
        P(None, "freq", None, "node"),
        P(),
        P(),
        P("freq", None, None, None),
        P("freq", None, None, None),
    )
    return jax.shard_map(
        shards, mesh=mesh, in_specs=placed, out_specs=P(None, "node", "freq"), check_vma=False
    )
```

profile of v0, /device:TPU:1, one launch (start us, length us, event | category | flops | bytes accessed | tf_op | source)
XLA Modules:
  0.0 300.7 jit_solution(7121167841357710657)
XLA Ops:
  6.5 6.8 %copy.72 = bf16[2,16,4,2048]{1,2,0,3:T(4,128)(2,1)} copy(bf16[2,16,4,2048]{3,2,1,0:T(4,128)(2,1)} %param.5) | data formatting | bytes 1048576 | tf_op args[0]
  13.4 6.5 %reshape.206 = bf16[8,2,16384]{2,1,0:T(2,128)(2,1)} reshape(bf16[2048,2,4,16]{3,2,1,0:T(4,128)(2,1)} %bitcast.65) | data formatting | bytes 1048576
  19.8 5.2 %all-to-all-start.1 = ((bf16[8,2,16384]{2,1,0:T(2,128)(2,1)}), bf16[8,2,16384]{2,1,0:T(2,128)(2,1)S(1)}, u32[]{:S(2)}, u32[]{:S(2)}) async-start(bf16[8,2,16384]{2,1,0:T(2,128)(2,1)} %reshape.206), calls=%async_computation.1 | async-start | bytes 1048576 | tf_op jit(solution)/shard_map/all_to_all | solution.py:47
  25.8 6.0 %all-to-all-done.1 = bf16[8,2,16384]{2,1,0:T(2,128)(2,1)S(1)} async-done(((bf16[8,2,16384]{2,1,0:T(2,128)(2,1)}), bf16[8,2,16384]{2,1,0:T(2,128)(2,1)S(1)}, u32[]{:S(2)}, u32[]{:S(2)}) %all-to-all-start.1) | async-done | bytes 524320 | tf_op jit(solution)/shard_map/all_to_all | solution.py:47
  31.8 4.1 %reshape.207 = bf16[2048,2,4,16]{3,2,1,0:T(4,128)(2,1)} reshape(bf16[8,2,16384]{2,1,0:T(2,128)(2,1)S(1)} %all-to-all-done.1) | data formatting | bytes 1048576
  35.8 4.6 %copy.89 = bf16[2,16,4,8,256]{4,3,1,2,0:T(8,128)(2,1)S(1)} copy(bf16[2,16,4,8,256]{1,2,0,4,3:T(4,128)(2,1)} %bitcast.64) | data formatting | bytes 1048576 | tf_op jit(solution)/shard_map/all_to_all | solution.py:47
  42.9 18.0 %reduce-window.6 = s32[64,8,128]{2,1,0:T(8,128)S(1)} reduce-window(s32[64,8,128]{2,1,0:T(8,128)S(1)} %fusion.25, s32[]{:T(128)} %constant.39.clone.1), window={size=1x1x128 pad=0_0x0_0x127_0}, to_apply=%region_0.0 | reduce-window | flops 8323072 | bytes 524292 | tf_op jit(solution)/shard_map/reduce-window
  61.6 4.3 %scatter_custom_fusion = s32[1536]{0:T(1024)S(1)} fusion(s32[1024]{0:T(1024)S(1)} %bitcast.77, s32[1024]{0:T(1024)S(1)} %iota.21, s32[]{:T(128)} %constant.31.clone.1), kind=kCustom, calls=%fused_computation.44 | custom fusion | bytes 6148 | tf_op jit(solution)/shard_map/scatter | solution.py:43
  66.1 24.4 %all-gather.2.cloned.1.call-done = bf16[2,128,4,1024]{1,2,3,0:T(4,128)(2,1)} async-done(((bf16[2,128,4,256]{1,2,3,0:T(4,128)(2,1)}), bf16[2,128,4,1024]{1,2,3,0:T(4,128)(2,1)}) %all-gather.2.cloned.1.call-update) | async-done | bytes 2097168 | tf_op jit(solution)/shard_map/all_gather | solution.py:63
  90.5 9.3 %gather_fusion.1 = bf16[1536,2,128,4]{2,3,1,0:T(4,128)(2,1)} fusion(bf16[2,128,4,1024]{1,2,3,0:T(4,128)(2,1)} %all-gather.2.cloned.1.call-done, s32[2048]{0:T(1024)S(1)} %pad_clamp_fusion), kind=kCustom, calls=%fused_computation.1 | custom fusion | bytes 6297600 | tf_op jit(solution)/shard_map/jit(_take)/gather | solution.py:64
  99.8 5.9 %copy.80 = bf16[2,128,4,1536]{3,2,1,0:T(4,128)(2,1)S(1)} copy(bf16[2,128,4,1536]{1,2,0,3:T(4,128)(2,1)} %bitcast.66) | data formatting | bytes 6291456 | tf_op jit(solution)/shard_map/jit(_take)/gather | solution.py:64
  105.8 23.4 %gather.15 = bf16[1024,8,8,24]{3,2,1,0:T(8,128)(2,1)} reshape(bf16[2,128,4,1536]{3,2,1,0:T(4,128)(2,1)S(1)} %copy.80) | data formatting | bytes 6291456 | tf_op jit(solution)/shard_map/jit(_take)/gather | solution.py:64
  129.2 13.9 %broadcast_select_fusion = bf16[1024,8,8,24]{3,2,1,0:T(8,128)(2,1)} fusion(bf16[1024,8,8,24]{3,2,1,0:T(8,128)(2,1)} %gather.15, pred[8,8,24]{2,1,0:T(8,128)(4,1)S(1)} %broadcast_in_dim.35), kind=kLoop, calls=%fused_computation.6 | loop fusion | flops 1572864 | bytes 6292992 | tf_op jit(solution)/shard_map/jit(_take)/select_n | solution.py:64
  143.1 17.3 %copy.81 = bf16[1024,8,8,24]{0,3,2,1:T(8,128)(2,1)} copy(bf16[1024,8,8,24]{3,2,1,0:T(8,128)(2,1)} %broadcast_select_fusion) | data formatting | bytes 6291456 | tf_op jit(solution)/shard_map/jit(_take)/select_n | solution.py:64
  160.3 4.6 %all-to-all-start.2 = ((bf16[1024,8,8,24]{0,3,2,1:T(8,128)(2,1)}), bf16[1024,8,8,24]{0,3,2,1:T(8,128)(2,1)S(1)}, u32[]{:S(2)}, u32[]{:S(2)}) async-start(bf16[1024,8,8,24]{0,3,2,1:T(8,128)(2,1)} %copy.81), calls=%async_computation.2 | async-start | bytes 6291456 | tf_op jit(solution)/shard_map/all_to_all | solution.py:67
  164.9 4.0 %gather_fusion = bf16[1536,128]{1,0:T(8,128)(2,1)} fusion(bf16[1024,128]{1,0:T(8,128)(2,1)S(1)} %bitcast.61, s32[2048]{0:T(1024)S(1)} %pad_clamp_fusion), kind=kCustom, calls=%fused_computation | custom fusion | bytes 792576 | tf_op jit(solution)/shard_map/jit(_take)/gather | solution.py:61
  168.9 2.0 select_bitcast_fusion
  170.9 28.4 %all-to-all-done.2 = bf16[1024,8,8,24]{0,3,2,1:T(8,128)(2,1)S(1)} async-done(((bf16[1024,8,8,24]{0,3,2,1:T(8,128)(2,1)}), bf16[1024,8,8,24]{0,3,2,1:T(8,128)(2,1)S(1)}, u32[]{:S(2)}, u32[]{:S(2)}) %all-to-all-start.2) | async-done | bytes 3145760 | tf_op jit(solution)/shard_map/all_to_all | solution.py:67
  199.3 7.4 %all-to-all-start = ((bf16[1,8,8,24,128]{4,3,2,0,1:T(8,128)(2,1)}), bf16[1,8,8,24,128]{4,3,2,0,1:T(8,128)(2,1)}, u32[]{:S(2)}, u32[]{:S(2)}) async-start(bf16[1,8,8,24,128]{4,3,2,0,1:T(8,128)(2,1)} %select_bitcast_fusion), calls=%async_computation | async-start | bytes 786432 | tf_op jit(solution)/shard_map/all_to_all | solution.py:68
  206.7 3.1 %cosine_convert_fusion = (bf16[128,1024]{1,0:T(8,128)(2,1)}, bf16[128,1024]{1,0:T(8,128)(2,1)}) fusion(s32[1024]{0:T(1024)S(1)} %iota_add_fusion, s32[128]{0:T(128)S(1)} %multiply_add_fusion), kind=kLoop, calls=%fused_computation.23 | loop fusion | flops 2228224 | bytes 528896 | tf_op jit(solution)/shard_map/convert.2
  209.9 23.3 %copy.82 = bf16[1024,8,8,24]{3,2,1,0:T(8,128)(2,1)} copy(bf16[1024,8,8,24]{0,3,2,1:T(8,128)(2,1)S(1)} %all-to-all-done.2) | data formatting | bytes 6291456 | tf_op jit(solution)/shard_map/all_to_all | solution.py:67
  233.2 41.2 %fusion.8 = bf16[4,1024,8,128]{1,3,0,2:T(8,128)(2,1)} fusion(bf16[256,4,8,8,24]{4,3,2,1,0:T(8,128)(2,1)} %bitcast.63, bf16[128,1024]{1,0:T(8,128)(2,1)} %get-tuple-element.10, bf16[128,1024]{1,0:T(8,128)(2,1)} %get-tuple-element.9, bf16[1,8,8,24,128]{4,3,2,0,1:T(8,128)(2,1)} %all-to-all-done), kind=kOutput, calls=%fused_computation.9 | convolution fusion | flops 4843372544 | bytes 12451840 | tf_op jit(solution)/shard_map/hskct,skcn->htkn/dot_general | solution.py:73
  274.3 8.2 %copy.84 = bf16[4,1024,8,128]{1,3,2,0:T(8,128)(2,1)} copy(bf16[4,1024,8,128]{1,3,0,2:T(8,128)(2,1)} %fusion.8) | data formatting | bytes 16777216 | tf_op jit(solution)/shard_map/convert_element_type | solution.py:77
  282.5 11.3 %copy.85 = bf16[4,1024,1024]{2,1,0:T(8,128)(2,1)} copy(bf16[4,1024,1024]{1,2,0:T(8,128)(2,1)} %bitcast.62) | data formatting | bytes 16777216 | tf_op jit(solution)/shard_map/convert_element_type | solution.py:77
  (34 shorter events, 3.9 us)
Async XLA Ops:
  6.5 158.4 %copy-start = (bf16[1,4,256,128]{3,2,1,0:T(8,128)(2,1)S(1)}, bf16[1,4,256,128]{3,2,1,0:T(8,128)(2,1)}, u32[]{:S(2)}) copy-start(bf16[1,4,256,128]{3,2,1,0:T(8,128)(2,1)} %param.9) | copy-start | bytes 786436
  6.5 34.8 %copy-start.2 = (f32[4,128]{1,0:T(4,128)S(1)}, f32[4,128]{1,0:T(4,128)}, u32[]{:S(2)}) copy-start(f32[4,128]{1,0:T(4,128)} %param.6) | copy-start | bytes 6148
  13.4 29.5 %copy-start.1 = (s32[1,4,256,1]{2,3,1,0:T(1,128)S(1)}, s32[1,4,256,1]{2,3,1,0:T(1,128)}, u32[]{:S(2)}) copy-start(s32[1,4,256,1]{2,3,1,0:T(1,128)} %param.8) | copy-start | bytes 12292
  19.8 12.0 %all-to-all-start.1 = ((bf16[8,2,16384]{2,1,0:T(2,128)(2,1)}), bf16[8,2,16384]{2,1,0:T(2,128)(2,1)S(1)}, u32[]{:S(2)}, u32[]{:S(2)}) async-start(bf16[8,2,16384]{2,1,0:T(2,128)(2,1)} %reshape.206), calls=%async_computation.1 | async-start | bytes 1048576 | tf_op jit(solution)/shard_map/all_to_all | solution.py:47
  25.1 65.4 %all-gather.2.cloned.1.call-start = ((), (), s32[]{:S(2)}) async-start(), calls=%async_computation.3 | async-start | bytes 2621440 | tf_op jit(solution)/shard_map/all_gather | solution.py:63
  160.3 39.0 %all-to-all-start.2 = ((bf16[1024,8,8,24]{0,3,2,1:T(8,128)(2,1)}), bf16[1024,8,8,24]{0,3,2,1:T(8,128)(2,1)S(1)}, u32[]{:S(2)}, u32[]{:S(2)}) async-start(bf16[1024,8,8,24]{0,3,2,1:T(8,128)(2,1)} %copy.81), calls=%async_computation.2 | async-start | bytes 6291456 | tf_op jit(solution)/shard_map/all_to_all | solution.py:67
  199.3 33.8 %all-to-all-start = ((bf16[1,8,8,24,128]{4,3,2,0,1:T(8,128)(2,1)}), bf16[1,8,8,24,128]{4,3,2,0,1:T(8,128)(2,1)}, u32[]{:S(2)}, u32[]{:S(2)}) async-start(bf16[1,8,8,24,128]{4,3,2,0,1:T(8,128)(2,1)} %select_bitcast_fusion), calls=%async_computation | async-start | bytes 786432 | tf_op jit(solution)/shard_map/all_to_all | solution.py:68
Sparse Core Ops, SparseCore 0:
  43.0 47.4 all-gather.1
where the time goes:
time: 303 us; the launch traced here: 301 us
  local copies, waits for them, and re-layouts  130 us (43%)
  waiting for transfers between devices  58.8 us (19%)
  matrix products  41.2 us (14%)
  other arithmetic  39.6 us (13%)
  starting transfers between devices  17.2 us (6%)
  between operations  13.6 us (4%)
    dot_general x1, matrix products, shards(): jnp.einsum('hskct,skcn->htkn', series, got_weight[0], preferred_element_t...  41.2 us
    gather x3, local copies, waits for them, and re-layouts, shards(): sent_spectra = jnp.take(spectra, members, axis=3, mode='fill', fill_value=0)  38.7 us
    all_to_all x1, waiting for transfers between devices, shards(): lax.all_to_all(sent_spectra, 'freq', split_axis=1, concat_axis=1, tiled=T...  28.4 us
    all_gather x1, waiting for transfers between devices, shards(): spectra = lax.all_gather(scaled, 'node', axis=3, tiled=True)  24.4 us
    all_to_all x1, local copies, waits for them, and re-layouts, shards(): lax.all_to_all(sent_spectra, 'freq', split_axis=1, concat_axis=1, tiled=T...  23.3 us
    another operation x5, other arithmetic  21.6 us
    convert_element_type x2, local copies, waits for them, and re-layouts, shards(): return node_loads.astype(jnp.bfloat16)  19.5 us
    unnamed x9, local copies, waits for them, and re-layouts  17.4 us
  transfers between devices with their start and end apart: 4, of which 3 were waited for; matrix products, arithmetic and copies ran while one was open for 19% of the time, Pallas kernels for 0%

commit v1 on v0

--- a/solution.py
+++ b/solution.py
@@ -1,8 +1,11 @@
+import functools
 import math
 
 import jax
 import jax.numpy as jnp
 from jax import lax
+from jax.experimental import pallas as pl
+from jax.experimental.pallas import tpu as pltpu
 from jax.sharding import PartitionSpec as P
 
 F = 128
@@ -10,6 +13,8 @@
 BIN_STEP = 15
 PHASE_LEVELS = 4096
 TILE_DEV = 8
+SLOT = 32
+MESH = pl.DeviceIdType.MESH
 
 
 def scale_spectra(pressure, spectrum_amp, phase_code):
@@ -32,6 +37,250 @@
     return jnp.concatenate([jnp.cos(turn_angle), -jnp.sin(turn_angle)], axis=0).astype(jnp.bfloat16)
 
 
+def basis_rows(first_step, step_count):
+    freq_bin = 1 + BIN_STEP * jnp.arange(F, dtype=jnp.int32)
+    step_ids = first_step + jnp.arange(step_count, dtype=jnp.int32)
+    turn_count = step_ids[:, None] * freq_bin[None, :] % TSTEPS
+    turn_angle = turn_count.astype(jnp.float32) * (2.0 * math.pi / TSTEPS)
+    return jnp.concatenate([jnp.cos(turn_angle), -jnp.sin(turn_angle)], axis=1).astype(jnp.bfloat16)
+
+
+def slot_rows(panel_tile):
+    tile_ids = panel_tile.reshape(-1)
+    count = tile_ids.shape[0]
+    order = jnp.arange(count, dtype=jnp.int32)
+    same = (tile_ids[:, None] == tile_ids[None, :]) & (order[:, None] < order[None, :])
+    rank = jnp.sum(same.astype(jnp.int32), axis=0)
+    return (tile_ids * SLOT + rank).reshape(1, count)
+
+
+def load_kernel(owners, windows, x_ref, w_ref, s_ref, out_ref, xall, wall, sall, pick, xs, ws, block, m,
+                z_send, z_recv, w_send, w_recv, s_send, s_recv, m_send, m_recv, own_sem):
+    me = lax.axis_index("freq")
+    z = lax.axis_index("node")
+    rows, panels = x_ref.shape
+    part = panels // owners
+    groups = xs.shape[0]
+    slots = groups * 128
+    per_group = 128 // SLOT
+    group_dev = groups // owners
+
+    barrier = pltpu.get_barrier_semaphore()
+    for d in range(1, owners):
+        pl.semaphore_signal(barrier, inc=1, device_id=(lax.rem(me + d, owners), z), device_id_type=MESH)
+    for d in range(1, windows):
+        pl.semaphore_signal(barrier, inc=1, device_id=(me, lax.rem(z + d, windows)), device_id_type=MESH)
+    pl.semaphore_wait(barrier, owners + windows - 2)
+
+    def z_copy(b, source, way, target):
+        return pltpu.make_async_remote_copy(
+            src_ref=source, dst_ref=xall.at[b], send_sem=z_send.at[way, b], recv_sem=z_recv.at[b],
+            device_id=(me, target), device_id_type=MESH)
+
+    def f_copy(source, dest, sends, recvs, d):
+        return pltpu.make_async_remote_copy(
+            src_ref=source, dst_ref=dest, send_sem=sends.at[d], recv_sem=recvs.at[d],
+            device_id=(lax.rem(me + d, owners), z), device_id_type=MESH)
+
+    @pl.when(z + 1 < windows)
+    def _():
+        z_copy(z, x_ref, 0, z + 1).start()
+
+    @pl.when(z > 0)
+    def _():
+        z_copy(z, x_ref, 1, z - 1).start()
+
+    for d in range(1, owners):
+        f_copy(s_ref, sall.at[me], s_send, s_recv, d).start()
+    for d in range(1, owners):
+        f_copy(w_ref, wall.at[me], w_send, w_recv, d).start()
+
+    sall[pl.ds(me, 1)] = s_ref[...][None]
+    wall[pl.ds(me, 1)] = w_ref[...][None]
+
+    for d in range(1, owners):
+        f_copy(s_ref, sall.at[lax.rem(me + owners - d, owners)], s_send, s_recv, d).wait_recv()
+
+    step = 256
+
+    def build(index, carry):
+        g = index // (slots // step)
+        first = pl.multiple_of(lax.rem(index, slots // step) * step, step)
+        ids = first + lax.broadcasted_iota(jnp.int32, (step, sall.shape[2]), 0)
+        pick[g, pl.ds(first, step)] = jnp.where(ids == sall[g], 1.0, 0.0).astype(jnp.bfloat16)
+        return carry
+
+    lax.fori_loop(0, owners * (slots // step), build, 0)
+
+    def place(source, b, fresh):
+        cols = pl.ds(pl.multiple_of(b * part, part), part)
+
+        def one(g, carry):
+            x = source[:, pl.ds(pl.multiple_of(g * part, part), part)]
+            got = lax.dot_general(x, pick[g, :, cols], (((1,), (1,)), ((), ())),
+                                  preferred_element_type=jnp.float32).astype(jnp.bfloat16)
+            lanes = pl.ds(pl.multiple_of(g * 128, 128), 128)
+            for u in range(groups):
+                piece = got[:, u * 128:(u + 1) * 128]
+                if fresh:
+                    xs[u, :, lanes] = piece
+                else:
+                    xs[u, :, lanes] = xs[u, :, lanes] + piece
+            return carry
+
+        lax.fori_loop(0, owners, one, 0)
+
+    def weigh(g):
+        lanes = pl.ds(pl.multiple_of(g * 128, 128), 128)
+
+        def one(index, carry):
+            first = pl.multiple_of(index * step, step)
+            got = jnp.dot(pick[g, pl.ds(first, step)], wall[g], preferred_element_type=jnp.float32)
+            got = got.astype(jnp.bfloat16)
+            for half in range(step // 128):
+                ws[index * (step // 128) + half, lanes] = got[half * 128:(half + 1) * 128]
+            return carry
+
+        lax.fori_loop(0, slots // step, one, 0)
+
+    def arrive(s):
+        low, high = z - s, z + s
+
+        @pl.when(low >= 0)
+        def _():
+            z_copy(low, xall.at[low], 0, z).wait_recv()
+
+            @pl.when(z + 1 < windows)
+            def _():
+                z_copy(low, xall.at[low], 0, z + 1).start()
+
+        @pl.when(high < windows)
+        def _():
+            z_copy(high, xall.at[high], 1, z).wait_recv()
+
+            @pl.when(z > 0)
+            def _():
+                z_copy(high, xall.at[high], 1, z - 1).start()
+
+        @pl.when(low >= 0)
+        def _():
+            place(xall.at[low], low, False)
+
+        @pl.when(high < windows)
+        def _():
+            place(xall.at[high], high, False)
+
+    place(x_ref, z, True)
+    for s in range(1, windows - 1):
+        arrive(s)
+    weigh(me)
+    for d in range(1, owners):
+        src = lax.rem(me + owners - d, owners)
+        f_copy(w_ref, wall.at[src], w_send, w_recv, d).wait_recv()
+        weigh(src)
+    arrive(windows - 1)
+
+    part_of = lax.rem(lax.broadcasted_iota(jnp.int32, (owners * 128, 128), 0) // SLOT, per_group)
+
+    def gather_loads(target):
+        def one(e, carry):
+            u = target * group_dev + e
+            w = ws[u]
+            for tt in range(per_group):
+                block[:, tt * 128:(tt + 1) * 128] = jnp.where(part_of == tt, w, jnp.zeros_like(w))
+            wide = per_group * 128
+            got = jnp.dot(xs[u], block[...], preferred_element_type=jnp.float32).astype(jnp.bfloat16)
+            m[target, :, :, :, pl.ds(pl.multiple_of(e * wide, wide), wide)] = got.reshape(m.shape[1:4] + (wide,))
+            return carry
+
+        lax.fori_loop(0, group_dev, one, 0)
+
+    def m_copy(d):
+        target = lax.rem(me + d, owners)
+        return pltpu.make_async_remote_copy(
+            src_ref=m.at[target], dst_ref=out_ref.at[:, :, me], send_sem=m_send.at[d], recv_sem=m_recv.at[d],
+            device_id=(target, z), device_id_type=MESH)
+
+    for d in range(1, owners):
+        gather_loads(lax.rem(me + d, owners))
+        m_copy(d).start()
+    gather_loads(me)
+    own = pltpu.make_async_copy(m.at[me], out_ref.at[:, :, me], own_sem)
+    own.start()
+    own.wait()
+
+    for d in range(1, owners):
+        src = lax.rem(me + owners - d, owners)
+        pltpu.make_async_remote_copy(
+            src_ref=m.at[src], dst_ref=out_ref.at[:, :, src], send_sem=m_send.at[d], recv_sem=m_recv.at[d],
+            device_id=(src, z), device_id_type=MESH).wait_recv()
+    for d in range(1, owners):
+        f_copy(s_ref, sall.at[me], s_send, s_recv, d).wait_send()
+        f_copy(w_ref, wall.at[me], w_send, w_recv, d).wait_send()
+        m_copy(d).wait_send()
+    for s in range(windows):
+        low, high = z - s, z + s
+
+        @pl.when((low >= 0) & (z + 1 < windows))
+        def _():
+            z_copy(low, x_ref, 0, z + 1).wait_send()
+
+        @pl.when((high < windows) & (z > 0))
+        def _():
+            z_copy(high, x_ref, 1, z - 1).wait_send()
+
+
+def node_spectra(x, w, s, owners, windows, headings, freqs):
+    rows, panels = x.shape
+    groups = owners * TILE_DEV * SLOT // 128
+    length = w.shape[0]
+    dma = pltpu.SemaphoreType.DMA
+    vmem = pl.BlockSpec(memory_space=pltpu.VMEM)
+    nodes = TILE_DEV * 128
+    return pl.pallas_call(
+        functools.partial(load_kernel, owners, windows),
+        out_shape=jax.ShapeDtypeStruct((headings, 2, owners, freqs, nodes), jnp.bfloat16),
+        in_specs=[vmem] * 3,
+        out_specs=vmem,
+        scratch_shapes=[
+            pltpu.VMEM((windows, rows, panels), jnp.bfloat16),
+            pltpu.VMEM((owners, length, 128), jnp.bfloat16),
+            pltpu.VMEM((owners, 1, length), jnp.int32),
+            pltpu.VMEM((owners, groups * 128, length), jnp.bfloat16),
+            pltpu.VMEM((groups, rows, owners * 128), jnp.bfloat16),
+            pltpu.VMEM((groups, owners * 128, 128), jnp.bfloat16),
+            pltpu.VMEM((owners * 128, 128 // SLOT * 128), jnp.bfloat16),
+            pltpu.VMEM((owners, headings, 2, freqs, nodes), jnp.bfloat16),
+            dma((2, windows)), dma((windows,)),
+            dma((owners,)), dma((owners,)), dma((owners,)), dma((owners,)), dma((owners,)), dma((owners,)),
+            dma(()),
+        ],
+        compiler_params=pltpu.CompilerParams(
+            collective_id=0, has_side_effects=True, vmem_limit_bytes=60 * 1024 * 1024),
+        name="node_spectra",
+    )(x, w, s)
+
+
+def series_kernel(basis_ref, m_ref, out_ref):
+    out_ref[0] = jnp.dot(basis_ref[...], m_ref[0], preferred_element_type=jnp.float32).astype(out_ref.dtype)
+
+
+def load_series(basis, m):
+    steps, depth = basis.shape
+    headings, _, nodes = m.shape
+    tall = 512
+    return pl.pallas_call(
+        series_kernel,
+        grid=(headings, steps // tall),
+        out_shape=jax.ShapeDtypeStruct((headings, steps, nodes), jnp.bfloat16),
+        in_specs=[pl.BlockSpec((tall, depth), lambda h, t: (t, 0)),
+                  pl.BlockSpec((1, depth, nodes), lambda h, t: (h, 0, 0))],
+        out_specs=pl.BlockSpec((1, tall, nodes), lambda h, t: (h, t, 0)),
+        compiler_params=pltpu.CompilerParams(vmem_limit_bytes=32 * 1024 * 1024),
+        name="load_series",
+    )(basis, m)
+
+
 def slot_members(tile_ids, tile_count, capacity):
     row_count = tile_ids.shape[0]
     onehot = (tile_ids[:, None] == jnp.arange(tile_count, dtype=jnp.int32)[None, :]).astype(
@@ -43,7 +292,7 @@
     return empty.at[slot_index].set(jnp.arange(row_count, dtype=jnp.int32))
 
 
-def shards(pressure, spectrum_amp, phase_code, panel_tile, patch_weight):
+def wide_shards(pressure, spectrum_amp, phase_code, panel_tile, patch_weight):
     regrouped = lax.all_to_all(pressure, "freq", split_axis=3, concat_axis=1, tiled=True)
     scaled = scale_spectra(regrouped, spectrum_amp, phase_code)
     freq_count = scaled.shape[1]
@@ -77,6 +326,26 @@
     return node_loads.astype(jnp.bfloat16)
 
 
+def shards(pressure, spectrum_amp, phase_code, panel_tile, patch_weight):
+    owners = lax.axis_size("freq")
+    windows = lax.axis_size("node")
+    length = panel_tile.shape[1] * panel_tile.shape[2]
+    capacity = 3 * length // (2 * TILE_DEV * owners)
+    pick_bytes = owners * owners * TILE_DEV * SLOT * length * 2
+    if capacity > SLOT or pick_bytes > 34 * 1024 * 1024:
+        return wide_shards(pressure, spectrum_amp, phase_code, panel_tile, patch_weight)
+    freqs, headings, panels = pressure.shape[1:]
+    first = lax.axis_index("freq") * freqs
+    amp = lax.dynamic_slice_in_dim(spectrum_amp, first, freqs, 1)
+    code = lax.dynamic_slice_in_dim(phase_code, first, freqs, 1)
+    scaled = scale_spectra(pressure, amp, code)
+    x = jnp.transpose(scaled, (2, 0, 1, 3)).reshape(headings * 2 * freqs, panels)
+    m = node_spectra(x, patch_weight.reshape(length, 128), slot_rows(panel_tile), owners, windows, headings, freqs)
+    window_len = TSTEPS // windows
+    basis = basis_rows(lax.axis_index("node") * window_len, window_len)
+    return load_series(basis, m.reshape(headings, 2 * F, TILE_DEV * 128))
+
+
 def solution(mesh):
     placed = (
         P(None, "freq", None, "node"),

time: 303 us -> 103 us (0.34)
  local copies, waits for them, and re-layouts: 130 us -> 2.92 us
  Pallas kernels: 0 us -> 91.6 us
  waiting for transfers between devices: 58.8 us -> 0 us
  matrix products: 41.2 us -> 0 us
  other arithmetic: 39.6 us -> 7.73 us
  starting transfers between devices: 17.2 us -> 0 us
  between operations: 13.6 us -> 0.06 us
    pallas_call x0 -> x2, Pallas kernels: none -> 91.6 us  [the longest x1 85.5 us: node_spectra(): pl.pallas_call(functools.partial(load_kernel, owners, windows), out_shape...]
    gather x4 -> x0, local copies, waits for them, and re-layouts: 42.8 us -> none  [the longest x3 38.7 us: shards(): sent_spectra = jnp.take(spectra, members, axis=3, mode='fill', fill_value=0)]
    dot_general x1 -> x0, matrix products: 41.2 us -> none  [shards(): jnp.einsum('hskct,skcn->htkn', series, got_weight[0], preferred_element_t...]
    all_to_all x3 -> x0, waiting for transfers between devices: 34.4 us -> none  [the longest x1 28.4 us: shards(): lax.all_to_all(sent_spectra, 'freq', split_axis=1, concat_axis=1, tiled=T...]
    all_to_all x2 -> x0, local copies, waits for them, and re-layouts: 27.9 us -> none  [the longest x1 23.3 us: shards(): lax.all_to_all(sent_spectra, 'freq', split_axis=1, concat_axis=1, tiled=T...]
    all_gather x1 -> x0, waiting for transfers between devices: 24.4 us -> none  [shards(): spectra = lax.all_gather(scaled, 'node', axis=3, tiled=True)]
    convert_element_type x6 -> x0, local copies, waits for them, and re-layouts: 20.3 us -> none  [the longest x2 19.5 us: shards(): return node_loads.astype(jnp.bfloat16)]
    another operation x6 -> x2, other arithmetic: 22.8 us -> 4.01 us
  transfers between devices with their start and end apart: 4 -> 0, of which waited for: 3 -> 0; matrix products, arithmetic and copies ran while one was open for 19% -> 0% of each run, Pallas kernels for 0% -> 0%
where the time goes in v1:
time: 103 us; the launch traced here: 102 us
  Pallas kernels  91.6 us (89%)
  other arithmetic  7.73 us (8%)
  local copies, waits for them, and re-layouts  2.92 us (3%)
    pallas_call x1, Pallas kernels, node_spectra(): pl.pallas_call(functools.partial(load_kernel, owners, windows), out_shape...  85.5 us
    pallas_call x1, Pallas kernels, load_series(): pl.pallas_call(series_kernel, grid=(headings, steps // tall), out_shape=j...  6.09 us
    another operation x2, other arithmetic  4.01 us

profile of v1, /device:TPU:1, one launch (start us, length us, event | category | flops | bytes accessed | tf_op | source)
XLA Modules:
  0.0 102.3 jit_solution(16034382373450881508)
XLA Ops:
  0.0 1.2 %convert_reduce_fusion = s32[1024]{0:T(1024)S(1)} fusion(s32[1024]{0:T(1024)} %bitcast.19), kind=kLoop, calls=%fused_computation | loop fusion | flops 5241856 | bytes 8192 | tf_op jit(solution)/shard_map/reduce_sum | solution.py:53
  1.2 0.7 broadcast_multiply_fusion
  1.9 0.6 add.51.s_ref
  2.5 0.8 cosine_bitcast_fusion
  3.3 0.1 copy.11
  3.4 0.1 copy.12
  3.5 0.1 copy.10
  3.5 1.5 %fusion.3 = (bf16[1,16,4,2048]{3,2,1,0:T(4,128)(2,1)S(1)}, bf16[1,16,4,2048]{3,2,1,0:T(4,128)(2,1)S(1)}) fusion(f32[16,4]{1,0:T(8,128)S(1)} %copy.12, f32[16,4]{1,0:T(8,128)S(1)} %copy.11, f32[16,4]{1,0:T(8,128)S(1)} %copy.10, bf16[2,16,4,2048]{3,2,1,0:T(4,128)(2,1)} %param.5), kind=kLoop, calls=%fused_computation.14 | loop fusion | flops 1572864 | bytes 1049344 | tf_op jit(solution)/shard_map/convert
  5.1 0.4 maximum_bitcast_fusion
  5.5 1.1 %copy.13 = bf16[4,2,16,2048]{3,2,1,0:T(8,128)(2,1)} copy(bf16[4,2,16,2048]{3,0,2,1:T(4,128)(2,1)S(1)} %maximum_bitcast_fusion) | data formatting | bytes 1048576 | tf_op jit(solution)/shard_map/transpose | solution.py:342
  6.5 2.5 %cosine_convert_fusion = (bf16[1024,128]{1,0:T(8,128)(2,1)S(1)}, bf16[1024,128]{1,0:T(8,128)(2,1)S(1)}) fusion(s32[128]{0:T(128)S(1)} %multiply_add_fusion, s32[1024]{0:T(1024)S(1)} %iota_add_fusion), kind=kLoop, calls=%fused_computation.24 | loop fusion | flops 2228224 | bytes 528896 | tf_op jit(solution)/shard_map/convert.2
  9.0 0.1 pad_maximum_fusion.basis_ref
  9.1 85.5 %node_spectra.1 = bf16[4,2,8,16,1024]{4,3,2,1,0:T(8,128)(2,1)} custom-call(bf16[128,2048]{1,0:T(8,128)(2,1)} %bitcast.15, bf16[1024,128]{1,0:T(8,128)(2,1)} %bitcast.16, s32[1,1024]{1,0:T(1,128)} %add.51.s_ref), custom_call_target="tpu_custom_call" | custom-call | tf_op jit(solution)/shard_map/node_spectra/pallas_call | solution.py:240
  94.6 0.0 copy-start
  94.6 1.6 %copy-done = bf16[4,2,8,16,1024]{4,3,2,1,0:T(8,128)(2,1)S(1)} copy-done((bf16[4,2,8,16,1024]{4,3,2,1,0:T(8,128)(2,1)S(1)}, bf16[4,2,8,16,1024]{4,3,2,1,0:T(8,128)(2,1)}, u32[]{:S(2)}) %copy-start) | copy-done | bytes 2097176
  96.2 6.1 %load_series.1 = bf16[4,1024,1024]{2,1,0:T(8,128)(2,1)} custom-call(bf16[1024,256]{1,0:T(8,128)(2,1)S(1)} %pad_maximum_fusion.basis_ref, bf16[4,256,1024]{2,1,0:T(8,128)(2,1)S(1)} %bitcast.14), custom_call_target="tpu_custom_call" | custom-call | tf_op jit(solution)/shard_map/load_series/pallas_call | solution.py:272
  (2 shorter events, 0.0 us)
Async XLA Ops:
  94.6 1.6 %copy-start = (bf16[4,2,8,16,1024]{4,3,2,1,0:T(8,128)(2,1)S(1)}, bf16[4,2,8,16,1024]{4,3,2,1,0:T(8,128)(2,1)}, u32[]{:S(2)}) copy-start(bf16[4,2,8,16,1024]{4,3,2,1,0:T(8,128)(2,1)} %node_spectra.1) | copy-start | bytes 6291460

commit v2 on v1

--- a/solution.py
+++ b/solution.py
@@ -54,16 +54,17 @@
     return (tile_ids * SLOT + rank).reshape(1, count)
 
 
-def load_kernel(owners, windows, x_ref, w_ref, s_ref, out_ref, xall, wall, sall, pick, xs, ws, block, m,
-                z_send, z_recv, w_send, w_recv, s_send, s_recv, m_send, m_recv, own_sem):
+def load_kernel(owners, windows, x_ref, w_ref, s_ref, out_ref, xall, sall, cols, xs, ws, block, m,
+                z_send, z_recv, w_send, w_recv, o_send, o_recv, s_send, s_recv, m_send, m_recv, own_sem):
     me = lax.axis_index("freq")
     z = lax.axis_index("node")
     rows, panels = x_ref.shape
     part = panels // owners
     groups = xs.shape[0]
-    slots = groups * 128
     per_group = 128 // SLOT
     group_dev = groups // owners
+    chips = owners // 2
+    other = me + 1 - 2 * lax.rem(me, 2)
 
     barrier = pltpu.get_barrier_semaphore()
     for d in range(1, owners):
@@ -77,10 +78,25 @@
             src_ref=source, dst_ref=xall.at[b], send_sem=z_send.at[way, b], recv_sem=z_recv.at[b],
             device_id=(me, target), device_id_type=MESH)
 
-    def f_copy(source, dest, sends, recvs, d):
-        return pltpu.make_async_remote_copy(
-            src_ref=source, dst_ref=dest, send_sem=sends.at[d], recv_sem=recvs.at[d],
+    def s_copy(g, d):
+        return pltpu.make_async_remote_copy(
+            src_ref=s_ref, dst_ref=sall.at[g], send_sem=s_send.at[d], recv_sem=s_recv.at[d],
             device_id=(lax.rem(me + d, owners), z), device_id_type=MESH)
+
+    def lanes_of(g):
+        return pl.ds(pl.multiple_of(g * 128, 128), 128)
+
+    def w_copy(g, d):
+        held = ws.at[:, lanes_of(g)]
+        return pltpu.make_async_remote_copy(
+            src_ref=held, dst_ref=held, send_sem=w_send.at[d], recv_sem=w_recv.at[d],
+            device_id=(lax.rem(me + 2 * d, owners), z), device_id_type=MESH)
+
+    def o_copy(g, d):
+        held = ws.at[:, lanes_of(g)]
+        return pltpu.make_async_remote_copy(
+            src_ref=held, dst_ref=held, send_sem=o_send.at[d], recv_sem=o_recv.at[d],
+            device_id=(other, z), device_id_type=MESH)
 
     @pl.when(z + 1 < windows)
     def _():
@@ -91,57 +107,54 @@
         z_copy(z, x_ref, 1, z - 1).start()
 
     for d in range(1, owners):
-        f_copy(s_ref, sall.at[me], s_send, s_recv, d).start()
-    for d in range(1, owners):
-        f_copy(w_ref, wall.at[me], w_send, w_recv, d).start()
-
+        s_copy(me, d).start()
     sall[pl.ds(me, 1)] = s_ref[...][None]
-    wall[pl.ds(me, 1)] = w_ref[...][None]
-
-    for d in range(1, owners):
-        f_copy(s_ref, sall.at[lax.rem(me + owners - d, owners)], s_send, s_recv, d).wait_recv()
-
-    step = 256
-
-    def build(index, carry):
-        g = index // (slots // step)
-        first = pl.multiple_of(lax.rem(index, slots // step) * step, step)
-        ids = first + lax.broadcasted_iota(jnp.int32, (step, sall.shape[2]), 0)
-        pick[g, pl.ds(first, step)] = jnp.where(ids == sall[g], 1.0, 0.0).astype(jnp.bfloat16)
+
+    def weigh(u, carry):
+        ids = u * 128 + lax.broadcasted_iota(jnp.int32, (128, s_ref.shape[1]), 0)
+        pick = jnp.where(ids == s_ref[...], 1.0, 0.0).astype(jnp.bfloat16)
+        ws[u, lanes_of(me)] = jnp.dot(pick, w_ref[...], preferred_element_type=jnp.float32).astype(jnp.bfloat16)
         return carry
 
-    lax.fori_loop(0, owners * (slots // step), build, 0)
+    lax.fori_loop(0, groups, weigh, 0)
+    for d in range(1, chips):
+        w_copy(me, d).start()
+    o_copy(me, 0).start()
+
+    for d in range(1, owners):
+        s_copy(lax.rem(me + owners - d, owners), d).wait_recv()
+
+    def column(g, carry):
+        row = sall[g].astype(jnp.float32)
+        for k in range(row.shape[1] // 128):
+            piece = jnp.broadcast_to(row[:, k * 128:(k + 1) * 128], (128, 128))
+            cols[g, k * 128:(k + 1) * 128] = piece.T
+        return carry
+
+    lax.fori_loop(0, owners, column, 0)
+
+    wide = 256 // 128
 
     def place(source, b, fresh):
-        cols = pl.ds(pl.multiple_of(b * part, part), part)
-
         def one(g, carry):
             x = source[:, pl.ds(pl.multiple_of(g * part, part), part)]
-            got = lax.dot_general(x, pick[g, :, cols], (((1,), (1,)), ((), ())),
-                                  preferred_element_type=jnp.float32).astype(jnp.bfloat16)
-            lanes = pl.ds(pl.multiple_of(g * 128, 128), 128)
-            for u in range(groups):
-                piece = got[:, u * 128:(u + 1) * 128]
-                if fresh:
-                    xs[u, :, lanes] = piece
-                else:
-                    xs[u, :, lanes] = xs[u, :, lanes] + piece
+            col = cols[g, pl.ds(pl.multiple_of(b * part, part), part)]
+            lane = lax.broadcasted_iota(jnp.int32, col.shape, 1).astype(jnp.float32)
+            lanes = lanes_of(g)
+            for u in range(0, groups, wide):
+                pick = jnp.concatenate(
+                    [jnp.where(col == lane + float((u + v) * 128), 1.0, 0.0).astype(jnp.bfloat16) for v in range(wide)],
+                    axis=1)
+                got = jnp.dot(x, pick, preferred_element_type=jnp.float32).astype(jnp.bfloat16)
+                for v in range(wide):
+                    piece = got[:, v * 128:(v + 1) * 128]
+                    if fresh:
+                        xs[u + v, :, lanes] = piece
+                    else:
+                        xs[u + v, :, lanes] = xs[u + v, :, lanes] + piece
             return carry
 
         lax.fori_loop(0, owners, one, 0)
-
-    def weigh(g):
-        lanes = pl.ds(pl.multiple_of(g * 128, 128), 128)
-
-        def one(index, carry):
-            first = pl.multiple_of(index * step, step)
-            got = jnp.dot(pick[g, pl.ds(first, step)], wall[g], preferred_element_type=jnp.float32)
-            got = got.astype(jnp.bfloat16)
-            for half in range(step // 128):
-                ws[index * (step // 128) + half, lanes] = got[half * 128:(half + 1) * 128]
-            return carry
-
-        lax.fori_loop(0, slots // step, one, 0)
 
     def arrive(s):
         low, high = z - s, z + s
@@ -162,6 +175,9 @@
             def _():
                 z_copy(high, xall.at[high], 1, z - 1).start()
 
+    def settle(s):
+        low, high = z - s, z + s
+
         @pl.when(low >= 0)
         def _():
             place(xall.at[low], low, False)
@@ -170,27 +186,42 @@
         def _():
             place(xall.at[high], high, False)
 
+    def spread():
+        part_of = lax.rem(lax.broadcasted_iota(jnp.int32, (128, 128), 0) // SLOT, per_group)
+
+        def one(u, carry):
+            for g in range(owners):
+                w = ws[u, g * 128:(g + 1) * 128]
+                for tt in range(per_group):
+                    block[u, g * 128:(g + 1) * 128, tt * 128:(tt + 1) * 128] = jnp.where(
+                        part_of == tt, w, jnp.zeros_like(w))
+            return carry
+
+        lax.fori_loop(0, groups, one, 0)
+
     place(x_ref, z, True)
-    for s in range(1, windows - 1):
+    arrive(1)
+    for d in range(1, chips):
+        src = lax.rem(me + owners - 2 * d, owners)
+        w_copy(src, d).wait_recv()
+        o_copy(src, d).start()
+    settle(1)
+    for s in range(2, windows - 1):
         arrive(s)
-    weigh(me)
-    for d in range(1, owners):
-        src = lax.rem(me + owners - d, owners)
-        f_copy(w_ref, wall.at[src], w_send, w_recv, d).wait_recv()
-        weigh(src)
-    arrive(windows - 1)
-
-    part_of = lax.rem(lax.broadcasted_iota(jnp.int32, (owners * 128, 128), 0) // SLOT, per_group)
+        settle(s)
+    for d in range(chips):
+        o_copy(lax.rem(other + owners - 2 * d, owners), d).wait_recv()
+    spread()
+    for s in range(max(2, windows - 1), windows):
+        arrive(s)
+        settle(s)
 
     def gather_loads(target):
         def one(e, carry):
             u = target * group_dev + e
-            w = ws[u]
-            for tt in range(per_group):
-                block[:, tt * 128:(tt + 1) * 128] = jnp.where(part_of == tt, w, jnp.zeros_like(w))
-            wide = per_group * 128
-            got = jnp.dot(xs[u], block[...], preferred_element_type=jnp.float32).astype(jnp.bfloat16)
-            m[target, :, :, :, pl.ds(pl.multiple_of(e * wide, wide), wide)] = got.reshape(m.shape[1:4] + (wide,))
+            width = per_group * 128
+            got = jnp.dot(xs[u], block[u], preferred_element_type=jnp.float32).astype(jnp.bfloat16)
+            m[target, :, :, :, pl.ds(pl.multiple_of(e * width, width), width)] = got.reshape(m.shape[1:4] + (width,))
             return carry
 
         lax.fori_loop(0, group_dev, one, 0)
@@ -215,9 +246,12 @@
             src_ref=m.at[src], dst_ref=out_ref.at[:, :, src], send_sem=m_send.at[d], recv_sem=m_recv.at[d],
             device_id=(src, z), device_id_type=MESH).wait_recv()
     for d in range(1, owners):
-        f_copy(s_ref, sall.at[me], s_send, s_recv, d).wait_send()
-        f_copy(w_ref, wall.at[me], w_send, w_recv, d).wait_send()
+        s_copy(me, d).wait_send()
         m_copy(d).wait_send()
+    for d in range(1, chips):
+        w_copy(me, d).wait_send()
+    for d in range(chips):
+        o_copy(me, d).wait_send()
     for s in range(windows):
         low, high = z - s, z + s
 
@@ -244,19 +278,19 @@
         out_specs=vmem,
         scratch_shapes=[
             pltpu.VMEM((windows, rows, panels), jnp.bfloat16),
-            pltpu.VMEM((owners, length, 128), jnp.bfloat16),
             pltpu.VMEM((owners, 1, length), jnp.int32),
-            pltpu.VMEM((owners, groups * 128, length), jnp.bfloat16),
+            pltpu.VMEM((owners, length, 128), jnp.float32),
             pltpu.VMEM((groups, rows, owners * 128), jnp.bfloat16),
             pltpu.VMEM((groups, owners * 128, 128), jnp.bfloat16),
-            pltpu.VMEM((owners * 128, 128 // SLOT * 128), jnp.bfloat16),
+            pltpu.VMEM((groups, owners * 128, 128 // SLOT * 128), jnp.bfloat16),
             pltpu.VMEM((owners, headings, 2, freqs, nodes), jnp.bfloat16),
             dma((2, windows)), dma((windows,)),
             dma((owners,)), dma((owners,)), dma((owners,)), dma((owners,)), dma((owners,)), dma((owners,)),
+            dma((owners,)), dma((owners,)),
             dma(()),
         ],
         compiler_params=pltpu.CompilerParams(
-            collective_id=0, has_side_effects=True, vmem_limit_bytes=60 * 1024 * 1024),
+            collective_id=0, has_side_effects=True, vmem_limit_bytes=56 * 1024 * 1024),
         name="node_spectra",
     )(x, w, s)
 
@@ -331,8 +365,8 @@
     windows = lax.axis_size("node")
     length = panel_tile.shape[1] * panel_tile.shape[2]
     capacity = 3 * length // (2 * TILE_DEV * owners)
-    pick_bytes = owners * owners * TILE_DEV * SLOT * length * 2
-    if capacity > SLOT or pick_bytes > 34 * 1024 * 1024:
+    block_bytes = owners * owners * TILE_DEV * SLOT * 128 * (128 // SLOT) * 2
+    if capacity > SLOT or block_bytes > 20 * 1024 * 1024:
         return wide_shards(pressure, spectrum_amp, phase_code, panel_tile, patch_weight)
     freqs, headings, panels = pressure.shape[1:]
     first = lax.axis_index("freq") * freqs

time: 103 us -> 98.4 us (0.955)
  Pallas kernels: 91.6 us -> 87.4 us
    pallas_call x1, Pallas kernels: 85.5 us -> 81.3 us  [node_spectra(): pl.pallas_call(functools.partial(load_kernel, owners, windows), out_shape...]
where the time goes in v2:
time: 98.4 us; the launch traced here: 98.1 us
  Pallas kernels  87.4 us (89%)
  other arithmetic  7.73 us (8%)
  local copies, waits for them, and re-layouts  2.92 us (3%)
    pallas_call x1, Pallas kernels, node_spectra(): pl.pallas_call(functools.partial(load_kernel, owners, windows), out_shape...  81.3 us
    pallas_call x1, Pallas kernels, load_series(): pl.pallas_call(series_kernel, grid=(headings, steps // tall), out_shape=j...  6.09 us
    another operation x2, other arithmetic  4.01 us

profile of v2, /device:TPU:1, one launch (start us, length us, event | category | flops | bytes accessed | tf_op | source)
XLA Modules:
  0.0 98.1 jit_solution(344141128381383431)
XLA Ops:
  0.0 1.2 %convert_reduce_fusion = s32[1024]{0:T(1024)S(1)} fusion(s32[1024]{0:T(1024)} %bitcast.19), kind=kLoop, calls=%fused_computation | loop fusion | flops 5241856 | bytes 8192 | tf_op jit(solution)/shard_map/reduce_sum | solution.py:53
  1.2 0.7 broadcast_multiply_fusion
  1.9 0.6 add.51.s_ref
  2.5 0.8 cosine_bitcast_fusion
  3.3 0.1 copy.11
  3.4 0.1 copy.12
  3.5 0.1 copy.10
  3.5 1.5 %fusion.3 = (bf16[1,16,4,2048]{3,2,1,0:T(4,128)(2,1)S(1)}, bf16[1,16,4,2048]{3,2,1,0:T(4,128)(2,1)S(1)}) fusion(f32[16,4]{1,0:T(8,128)S(1)} %copy.12, f32[16,4]{1,0:T(8,128)S(1)} %copy.11, f32[16,4]{1,0:T(8,128)S(1)} %copy.10, bf16[2,16,4,2048]{3,2,1,0:T(4,128)(2,1)} %param.5), kind=kLoop, calls=%fused_computation.14 | loop fusion | flops 1572864 | bytes 1049344 | tf_op jit(solution)/shard_map/convert
  5.1 0.4 maximum_bitcast_fusion
  5.5 1.1 %copy.13 = bf16[4,2,16,2048]{3,2,1,0:T(8,128)(2,1)} copy(bf16[4,2,16,2048]{3,0,2,1:T(4,128)(2,1)S(1)} %maximum_bitcast_fusion) | data formatting | bytes 1048576 | tf_op jit(solution)/shard_map/transpose | solution.py:376
  6.5 2.5 %cosine_convert_fusion = (bf16[1024,128]{1,0:T(8,128)(2,1)S(1)}, bf16[1024,128]{1,0:T(8,128)(2,1)S(1)}) fusion(s32[128]{0:T(128)S(1)} %multiply_add_fusion, s32[1024]{0:T(1024)S(1)} %iota_add_fusion), kind=kLoop, calls=%fused_computation.24 | loop fusion | flops 2228224 | bytes 528896 | tf_op jit(solution)/shard_map/convert.2
  9.0 0.1 pad_maximum_fusion.basis_ref
  9.1 81.3 %node_spectra.1 = bf16[4,2,8,16,1024]{4,3,2,1,0:T(8,128)(2,1)} custom-call(bf16[128,2048]{1,0:T(8,128)(2,1)} %bitcast.15, bf16[1024,128]{1,0:T(8,128)(2,1)} %bitcast.16, s32[1,1024]{1,0:T(1,128)} %add.51.s_ref), custom_call_target="tpu_custom_call" | custom-call | tf_op jit(solution)/shard_map/node_spectra/pallas_call | solution.py:274
  90.4 0.0 copy-start
  90.4 1.6 %copy-done = bf16[4,2,8,16,1024]{4,3,2,1,0:T(8,128)(2,1)S(1)} copy-done((bf16[4,2,8,16,1024]{4,3,2,1,0:T(8,128)(2,1)S(1)}, bf16[4,2,8,16,1024]{4,3,2,1,0:T(8,128)(2,1)}, u32[]{:S(2)}) %copy-start) | copy-done | bytes 2097176
  92.0 6.1 %load_series.1 = bf16[4,1024,1024]{2,1,0:T(8,128)(2,1)} custom-call(bf16[1024,256]{1,0:T(8,128)(2,1)S(1)} %pad_maximum_fusion.basis_ref, bf16[4,256,1024]{2,1,0:T(8,128)(2,1)S(1)} %bitcast.14), custom_call_target="tpu_custom_call" | custom-call | tf_op jit(solution)/shard_map/load_series/pallas_call | solution.py:306
  (2 shorter events, 0.0 us)
Async XLA Ops:
  90.4 1.6 %copy-start = (bf16[4,2,8,16,1024]{4,3,2,1,0:T(8,128)(2,1)S(1)}, bf16[4,2,8,16,1024]{4,3,2,1,0:T(8,128)(2,1)}, u32[]{:S(2)}) copy-start(bf16[4,2,8,16,1024]{4,3,2,1,0:T(8,128)(2,1)} %node_spectra.1) | copy-start | bytes 6291460

commit v3 on v2

--- a/solution.py
+++ b/solution.py
@@ -73,10 +73,24 @@
         pl.semaphore_signal(barrier, inc=1, device_id=(me, lax.rem(z + d, windows)), device_id_type=MESH)
     pl.semaphore_wait(barrier, owners + windows - 2)
 
-    def z_copy(b, source, way, target):
+    headings = m.shape[1]
+    each = rows // headings
+    cuts = [0, headings // 2, headings] if headings > 1 else [0, headings]
+    chunks = len(cuts) - 1
+
+    def rows_of(c):
+        return slice(cuts[c] * each, cuts[c + 1] * each)
+
+    def z_copy(c, b, source, way, target):
         return pltpu.make_async_remote_copy(
-            src_ref=source, dst_ref=xall.at[b], send_sem=z_send.at[way, b], recv_sem=z_recv.at[b],
-            device_id=(me, target), device_id_type=MESH)
+            src_ref=source.at[rows_of(c)], dst_ref=xall.at[b, rows_of(c)], send_sem=z_send.at[way, c, b],
+            recv_sem=z_recv.at[c, b], device_id=(me, target), device_id_type=MESH)
+
+    def own_up(c):
+        z_copy(c, z, x_ref, 0, z + 1).start()
+
+    def own_down(c):
+        z_copy(c, z, x_ref, 1, z - 1).start()
 
     def s_copy(g, d):
         return pltpu.make_async_remote_copy(
@@ -100,11 +114,11 @@
 
     @pl.when(z + 1 < windows)
     def _():
-        z_copy(z, x_ref, 0, z + 1).start()
+        own_up(0)
 
     @pl.when(z > 0)
     def _():
-        z_copy(z, x_ref, 1, z - 1).start()
+        own_down(0)
 
     for d in range(1, owners):
         s_copy(me, d).start()
@@ -135,9 +149,11 @@
 
     wide = 256 // 128
 
-    def place(source, b, fresh):
+    def place(c, source, b, fresh):
+        held = rows_of(c)
+
         def one(g, carry):
-            x = source[:, pl.ds(pl.multiple_of(g * part, part), part)]
+            x = source[held, pl.ds(pl.multiple_of(g * part, part), part)]
             col = cols[g, pl.ds(pl.multiple_of(b * part, part), part)]
             lane = lax.broadcasted_iota(jnp.int32, col.shape, 1).astype(jnp.float32)
             lanes = lanes_of(g)
@@ -149,42 +165,57 @@
                 for v in range(wide):
                     piece = got[:, v * 128:(v + 1) * 128]
                     if fresh:
-                        xs[u + v, :, lanes] = piece
+                        xs[u + v, held, lanes] = piece
                     else:
-                        xs[u + v, :, lanes] = xs[u + v, :, lanes] + piece
+                        xs[u + v, held, lanes] = xs[u + v, held, lanes] + piece
             return carry
 
         lax.fori_loop(0, owners, one, 0)
 
-    def arrive(s):
+    def arrive(c, s):
         low, high = z - s, z + s
 
         @pl.when(low >= 0)
         def _():
-            z_copy(low, xall.at[low], 0, z).wait_recv()
+            z_copy(c, low, xall.at[low], 0, z).wait_recv()
 
             @pl.when(z + 1 < windows)
             def _():
-                z_copy(low, xall.at[low], 0, z + 1).start()
+                z_copy(c, low, xall.at[low], 0, z + 1).start()
 
         @pl.when(high < windows)
         def _():
-            z_copy(high, xall.at[high], 1, z).wait_recv()
+            z_copy(c, high, xall.at[high], 1, z).wait_recv()
 
             @pl.when(z > 0)
             def _():
-                z_copy(high, xall.at[high], 1, z - 1).start()
-
-    def settle(s):
+                z_copy(c, high, xall.at[high], 1, z - 1).start()
+
+        if c + 1 < chunks:
+            up_now = z == s
+            down_now = windows - 1 - z == s
+            if s == 1:
+                up_now = up_now | (z == 0)
+                down_now = down_now | (z == windows - 1)
+
+            @pl.when(up_now & (z + 1 < windows))
+            def _():
+                own_up(c + 1)
+
+            @pl.when(down_now & (z > 0))
+            def _():
+                own_down(c + 1)
+
+    def settle(c, s):
         low, high = z - s, z + s
 
         @pl.when(low >= 0)
         def _():
-            place(xall.at[low], low, False)
+            place(c, xall.at[low], low, False)
 
         @pl.when(high < windows)
         def _():
-            place(xall.at[high], high, False)
+            place(c, xall.at[high], high, False)
 
     def spread():
         part_of = lax.rem(lax.broadcasted_iota(jnp.int32, (128, 128), 0) // SLOT, per_group)
@@ -199,55 +230,64 @@
 
         lax.fori_loop(0, groups, one, 0)
 
-    place(x_ref, z, True)
-    arrive(1)
-    for d in range(1, chips):
-        src = lax.rem(me + owners - 2 * d, owners)
-        w_copy(src, d).wait_recv()
-        o_copy(src, d).start()
-    settle(1)
-    for s in range(2, windows - 1):
-        arrive(s)
-        settle(s)
-    for d in range(chips):
-        o_copy(lax.rem(other + owners - 2 * d, owners), d).wait_recv()
-    spread()
-    for s in range(max(2, windows - 1), windows):
-        arrive(s)
-        settle(s)
-
-    def gather_loads(target):
+    def gather_loads(c, target):
         def one(e, carry):
             u = target * group_dev + e
             width = per_group * 128
-            got = jnp.dot(xs[u], block[u], preferred_element_type=jnp.float32).astype(jnp.bfloat16)
-            m[target, :, :, :, pl.ds(pl.multiple_of(e * width, width), width)] = got.reshape(m.shape[1:4] + (width,))
+            got = jnp.dot(xs[u, rows_of(c)], block[u], preferred_element_type=jnp.float32).astype(jnp.bfloat16)
+            m[target, cuts[c]:cuts[c + 1], :, :, pl.ds(pl.multiple_of(e * width, width), width)] = got.reshape(
+                (cuts[c + 1] - cuts[c],) + m.shape[2:4] + (width,))
             return carry
 
         lax.fori_loop(0, group_dev, one, 0)
 
-    def m_copy(d):
+    def m_copy(c, d, source, dest, device):
+        return pltpu.make_async_remote_copy(
+            src_ref=m.at[source, cuts[c]:cuts[c + 1]], dst_ref=out_ref.at[cuts[c]:cuts[c + 1], :, dest],
+            send_sem=m_send.at[c, d], recv_sem=m_recv.at[c, d], device_id=(device, z), device_id_type=MESH)
+
+    def sent(c, d):
         target = lax.rem(me + d, owners)
-        return pltpu.make_async_remote_copy(
-            src_ref=m.at[target], dst_ref=out_ref.at[:, :, me], send_sem=m_send.at[d], recv_sem=m_recv.at[d],
-            device_id=(target, z), device_id_type=MESH)
-
-    for d in range(1, owners):
-        gather_loads(lax.rem(me + d, owners))
-        m_copy(d).start()
-    gather_loads(me)
+        return m_copy(c, d, target, me, target)
+
+    def hand_out(c):
+        for d in range(1, owners):
+            gather_loads(c, lax.rem(me + d, owners))
+            sent(c, d).start()
+        gather_loads(c, me)
+
+    for c in range(chunks):
+        place(c, x_ref, z, True)
+        for s in range(1, windows):
+            arrive(c, s)
+            if c == 1 and s == 1:
+                for d in range(chips):
+                    o_copy(lax.rem(other + owners - 2 * d, owners), d).wait_recv()
+                spread()
+                hand_out(0)
+            settle(c, s)
+        if c == 0:
+            for d in range(1, chips):
+                src = lax.rem(me + owners - 2 * d, owners)
+                w_copy(src, d).wait_recv()
+                o_copy(src, d).start()
+        if chunks == 1:
+            for d in range(chips):
+                o_copy(lax.rem(other + owners - 2 * d, owners), d).wait_recv()
+            spread()
+        if c or chunks == 1:
+            hand_out(c)
     own = pltpu.make_async_copy(m.at[me], out_ref.at[:, :, me], own_sem)
     own.start()
     own.wait()
 
-    for d in range(1, owners):
-        src = lax.rem(me + owners - d, owners)
-        pltpu.make_async_remote_copy(
-            src_ref=m.at[src], dst_ref=out_ref.at[:, :, src], send_sem=m_send.at[d], recv_sem=m_recv.at[d],
-            device_id=(src, z), device_id_type=MESH).wait_recv()
+    for c in range(chunks):
+        for d in range(1, owners):
+            src = lax.rem(me + owners - d, owners)
+            m_copy(c, d, src, src, src).wait_recv()
+            sent(c, d).wait_send()
     for d in range(1, owners):
         s_copy(me, d).wait_send()
-        m_copy(d).wait_send()
     for d in range(1, chips):
         w_copy(me, d).wait_send()
     for d in range(chips):
@@ -257,11 +297,13 @@
 
         @pl.when((low >= 0) & (z + 1 < windows))
         def _():
-            z_copy(low, x_ref, 0, z + 1).wait_send()
+            for c in range(chunks):
+                z_copy(c, low, x_ref, 0, z + 1).wait_send()
 
         @pl.when((high < windows) & (z > 0))
         def _():
-            z_copy(high, x_ref, 1, z - 1).wait_send()
+            for c in range(chunks):
+                z_copy(c, high, x_ref, 1, z - 1).wait_send()
 
 
 def node_spectra(x, w, s, owners, windows, headings, freqs):
@@ -284,9 +326,9 @@
             pltpu.VMEM((groups, owners * 128, 128), jnp.bfloat16),
             pltpu.VMEM((groups, owners * 128, 128 // SLOT * 128), jnp.bfloat16),
             pltpu.VMEM((owners, headings, 2, freqs, nodes), jnp.bfloat16),
-            dma((2, windows)), dma((windows,)),
+            dma((2, headings, windows)), dma((headings, windows)),
             dma((owners,)), dma((owners,)), dma((owners,)), dma((owners,)), dma((owners,)), dma((owners,)),
-            dma((owners,)), dma((owners,)),
+            dma((headings, owners)), dma((headings, owners)),
             dma(()),
         ],
         compiler_params=pltpu.CompilerParams(

time: 98.4 us -> 90.3 us (0.918)
  Pallas kernels: 87.4 us -> 79.3 us
    pallas_call x1, Pallas kernels: 81.3 us -> 73.2 us  [node_spectra(): pl.pallas_call(functools.partial(load_kernel, owners, windows), out_shape...]
where the time goes in v3:
time: 90.3 us; the launch traced here: 90 us
  Pallas kernels  79.3 us (88%)
  other arithmetic  7.73 us (9%)
  local copies, waits for them, and re-layouts  2.92 us (3%)
    pallas_call x1, Pallas kernels, node_spectra(): pl.pallas_call(functools.partial(load_kernel, owners, windows), out_shape...  73.2 us
    pallas_call x1, Pallas kernels, load_series(): pl.pallas_call(series_kernel, grid=(headings, steps // tall), out_shape=j...  6.09 us
    another operation x2, other arithmetic  4.01 us

profile of v3, /device:TPU:1, one launch (start us, length us, event | category | flops | bytes accessed | tf_op | source)
XLA Modules:
  0.0 90.0 jit_solution(4213889580087437381)
XLA Ops:
  0.0 1.2 %convert_reduce_fusion = s32[1024]{0:T(1024)S(1)} fusion(s32[1024]{0:T(1024)} %bitcast.19), kind=kLoop, calls=%fused_computation | loop fusion | flops 5241856 | bytes 8192 | tf_op jit(solution)/shard_map/reduce_sum | solution.py:53
  1.2 0.7 broadcast_multiply_fusion
  1.9 0.6 add.51.s_ref
  2.5 0.8 cosine_bitcast_fusion
  3.3 0.1 copy.11
  3.4 0.1 copy.12
  3.5 0.1 copy.10
  3.5 1.5 %fusion.3 = (bf16[1,16,4,2048]{3,2,1,0:T(4,128)(2,1)S(1)}, bf16[1,16,4,2048]{3,2,1,0:T(4,128)(2,1)S(1)}) fusion(f32[16,4]{1,0:T(8,128)S(1)} %copy.12, f32[16,4]{1,0:T(8,128)S(1)} %copy.11, f32[16,4]{1,0:T(8,128)S(1)} %copy.10, bf16[2,16,4,2048]{3,2,1,0:T(4,128)(2,1)} %param.5), kind=kLoop, calls=%fused_computation.14 | loop fusion | flops 1572864 | bytes 1049344 | tf_op jit(solution)/shard_map/convert
  5.1 0.4 maximum_bitcast_fusion
  5.5 1.1 %copy.13 = bf16[4,2,16,2048]{3,2,1,0:T(8,128)(2,1)} copy(bf16[4,2,16,2048]{3,0,2,1:T(4,128)(2,1)S(1)} %maximum_bitcast_fusion) | data formatting | bytes 1048576 | tf_op jit(solution)/shard_map/transpose | solution.py:418
  6.5 2.5 %cosine_convert_fusion = (bf16[1024,128]{1,0:T(8,128)(2,1)S(1)}, bf16[1024,128]{1,0:T(8,128)(2,1)S(1)}) fusion(s32[128]{0:T(128)S(1)} %multiply_add_fusion, s32[1024]{0:T(1024)S(1)} %iota_add_fusion), kind=kLoop, calls=%fused_computation.24 | loop fusion | flops 2228224 | bytes 528896 | tf_op jit(solution)/shard_map/convert.2
  9.0 0.1 pad_maximum_fusion.basis_ref
  9.1 73.2 %node_spectra.1 = bf16[4,2,8,16,1024]{4,3,2,1,0:T(8,128)(2,1)} custom-call(bf16[128,2048]{1,0:T(8,128)(2,1)} %bitcast.15, bf16[1024,128]{1,0:T(8,128)(2,1)} %bitcast.16, s32[1,1024]{1,0:T(1,128)} %add.51.s_ref), custom_call_target="tpu_custom_call" | custom-call | tf_op jit(solution)/shard_map/node_spectra/pallas_call | solution.py:316
  82.4 0.0 copy-start
  82.4 1.6 %copy-done = bf16[4,2,8,16,1024]{4,3,2,1,0:T(8,128)(2,1)S(1)} copy-done((bf16[4,2,8,16,1024]{4,3,2,1,0:T(8,128)(2,1)S(1)}, bf16[4,2,8,16,1024]{4,3,2,1,0:T(8,128)(2,1)}, u32[]{:S(2)}) %copy-start) | copy-done | bytes 2097176
  83.9 6.1 %load_series.1 = bf16[4,1024,1024]{2,1,0:T(8,128)(2,1)} custom-call(bf16[1024,256]{1,0:T(8,128)(2,1)S(1)} %pad_maximum_fusion.basis_ref, bf16[4,256,1024]{2,1,0:T(8,128)(2,1)S(1)} %bitcast.14), custom_call_target="tpu_custom_call" | custom-call | tf_op jit(solution)/shard_map/load_series/pallas_call | solution.py:348
  (2 shorter events, 0.0 us)
Async XLA Ops:
  82.4 1.6 %copy-start = (bf16[4,2,8,16,1024]{4,3,2,1,0:T(8,128)(2,1)S(1)}, bf16[4,2,8,16,1024]{4,3,2,1,0:T(8,128)(2,1)}, u32[]{:S(2)}) copy-start(bf16[4,2,8,16,1024]{4,3,2,1,0:T(8,128)(2,1)} %node_spectra.1) | copy-start | bytes 6291460

commit v4 on v3

--- a/solution.py
+++ b/solution.py
@@ -142,7 +142,10 @@
         row = sall[g].astype(jnp.float32)
         for k in range(row.shape[1] // 128):
             piece = jnp.broadcast_to(row[:, k * 128:(k + 1) * 128], (128, 128))
-            cols[g, k * 128:(k + 1) * 128] = piece.T
+            group = jnp.floor(piece * (1.0 / 128.0)).T
+            place_in = piece.T - 128.0 * group
+            lane = lax.broadcasted_iota(jnp.int32, (128, 128), 1).astype(jnp.float32)
+            cols[g, k * 128:(k + 1) * 128] = jnp.where(place_in == lane, group, -1.0).astype(jnp.bfloat16)
         return carry
 
     lax.fori_loop(0, owners, column, 0)
@@ -155,11 +158,11 @@
         def one(g, carry):
             x = source[held, pl.ds(pl.multiple_of(g * part, part), part)]
             col = cols[g, pl.ds(pl.multiple_of(b * part, part), part)]
-            lane = lax.broadcasted_iota(jnp.int32, col.shape, 1).astype(jnp.float32)
             lanes = lanes_of(g)
+            one_hot, empty = jnp.ones_like(col), jnp.zeros_like(col)
             for u in range(0, groups, wide):
                 pick = jnp.concatenate(
-                    [jnp.where(col == lane + float((u + v) * 128), 1.0, 0.0).astype(jnp.bfloat16) for v in range(wide)],
+                    [jnp.where(col == jnp.bfloat16(u + v), one_hot, empty) for v in range(wide)],
                     axis=1)
                 got = jnp.dot(x, pick, preferred_element_type=jnp.float32).astype(jnp.bfloat16)
                 for v in range(wide):
@@ -250,11 +253,12 @@
         target = lax.rem(me + d, owners)
         return m_copy(c, d, target, me, target)
 
-    def hand_out(c):
-        for d in range(1, owners):
+    def hand_out(c, first, last):
+        for d in range(max(first, 1), last):
             gather_loads(c, lax.rem(me + d, owners))
             sent(c, d).start()
-        gather_loads(c, me)
+        if last == owners:
+            gather_loads(c, me)
 
     for c in range(chunks):
         place(c, x_ref, z, True)
@@ -264,7 +268,13 @@
                 for d in range(chips):
                     o_copy(lax.rem(other + owners - 2 * d, owners), d).wait_recv()
                 spread()
-                hand_out(0)
+                hand_out(0, 1, owners // 2)
+                if windows > 2:
+                    continue
+            if c == 1 and s == min(2, windows - 1):
+                hand_out(0, owners // 2, owners)
+                if s == 2:
+                    settle(c, 1)
             settle(c, s)
         if c == 0:
             for d in range(1, chips):
@@ -276,7 +286,7 @@
                 o_copy(lax.rem(other + owners - 2 * d, owners), d).wait_recv()
             spread()
         if c or chunks == 1:
-            hand_out(c)
+            hand_out(c, 1, owners)
     own = pltpu.make_async_copy(m.at[me], out_ref.at[:, :, me], own_sem)
     own.start()
     own.wait()
@@ -321,7 +331,7 @@
         scratch_shapes=[
             pltpu.VMEM((windows, rows, panels), jnp.bfloat16),
             pltpu.VMEM((owners, 1, length), jnp.int32),
-            pltpu.VMEM((owners, length, 128), jnp.float32),
+            pltpu.VMEM((owners, length, 128), jnp.bfloat16),
             pltpu.VMEM((groups, rows, owners * 128), jnp.bfloat16),
             pltpu.VMEM((groups, owners * 128, 128), jnp.bfloat16),
             pltpu.VMEM((groups, owners * 128, 128 // SLOT * 128), jnp.bfloat16),
@@ -408,7 +418,7 @@
     length = panel_tile.shape[1] * panel_tile.shape[2]
     capacity = 3 * length // (2 * TILE_DEV * owners)
     block_bytes = owners * owners * TILE_DEV * SLOT * 128 * (128 // SLOT) * 2
-    if capacity > SLOT or block_bytes > 20 * 1024 * 1024:
+    if capacity > SLOT or block_bytes > 20 * 1024 * 1024 or owners * TILE_DEV * SLOT > 128 * 256:
         return wide_shards(pressure, spectrum_amp, phase_code, panel_tile, patch_weight)
     freqs, headings, panels = pressure.shape[1:]
     first = lax.axis_index("freq") * freqs

time: 90.3 us -> 88.1 us (0.976)
  Pallas kernels: 79.3 us -> 77.1 us
    pallas_call x1, Pallas kernels: 73.2 us -> 71 us  [node_spectra(): pl.pallas_call(functools.partial(load_kernel, owners, windows), out_shape...]
where the time goes in v4:
time: 88.1 us; the launch traced here: 87.8 us
  Pallas kernels  77.1 us (88%)
  other arithmetic  7.73 us (9%)
  local copies, waits for them, and re-layouts  2.92 us (3%)
    pallas_call x1, Pallas kernels, node_spectra(): pl.pallas_call(functools.partial(load_kernel, owners, windows), out_shape...  71 us
    pallas_call x1, Pallas kernels, load_series(): pl.pallas_call(series_kernel, grid=(headings, steps // tall), out_shape=j...  6.09 us
    another operation x2, other arithmetic  4.01 us

profile of v4, /device:TPU:1, one launch (start us, length us, event | category | flops | bytes accessed | tf_op | source)
XLA Modules:
  0.0 87.8 jit_solution(10781411809948141005)
XLA Ops:
  0.0 1.2 %convert_reduce_fusion = s32[1024]{0:T(1024)S(1)} fusion(s32[1024]{0:T(1024)} %bitcast.19), kind=kLoop, calls=%fused_computation | loop fusion | flops 5241856 | bytes 8192 | tf_op jit(solution)/shard_map/reduce_sum | solution.py:53
  1.2 0.7 broadcast_multiply_fusion
  1.9 0.6 add.51.s_ref
  2.5 0.8 cosine_bitcast_fusion
  3.3 0.1 copy.11
  3.4 0.1 copy.12
  3.5 0.1 copy.10
  3.5 1.5 %fusion.3 = (bf16[1,16,4,2048]{3,2,1,0:T(4,128)(2,1)S(1)}, bf16[1,16,4,2048]{3,2,1,0:T(4,128)(2,1)S(1)}) fusion(f32[16,4]{1,0:T(8,128)S(1)} %copy.12, f32[16,4]{1,0:T(8,128)S(1)} %copy.11, f32[16,4]{1,0:T(8,128)S(1)} %copy.10, bf16[2,16,4,2048]{3,2,1,0:T(4,128)(2,1)} %param.5), kind=kLoop, calls=%fused_computation.14 | loop fusion | flops 1572864 | bytes 1049344 | tf_op jit(solution)/shard_map/convert
  5.1 0.4 maximum_bitcast_fusion
  5.5 1.1 %copy.13 = bf16[4,2,16,2048]{3,2,1,0:T(8,128)(2,1)} copy(bf16[4,2,16,2048]{3,0,2,1:T(4,128)(2,1)S(1)} %maximum_bitcast_fusion) | data formatting | bytes 1048576 | tf_op jit(solution)/shard_map/transpose | solution.py:428
  6.5 2.5 %cosine_convert_fusion = (bf16[1024,128]{1,0:T(8,128)(2,1)S(1)}, bf16[1024,128]{1,0:T(8,128)(2,1)S(1)}) fusion(s32[128]{0:T(128)S(1)} %multiply_add_fusion, s32[1024]{0:T(1024)S(1)} %iota_add_fusion), kind=kLoop, calls=%fused_computation.24 | loop fusion | flops 2228224 | bytes 528896 | tf_op jit(solution)/shard_map/convert.2
  9.0 0.1 pad_maximum_fusion.basis_ref
  9.1 71.0 %node_spectra.1 = bf16[4,2,8,16,1024]{4,3,2,1,0:T(8,128)(2,1)} custom-call(bf16[128,2048]{1,0:T(8,128)(2,1)} %bitcast.15, bf16[1024,128]{1,0:T(8,128)(2,1)} %bitcast.16, s32[1,1024]{1,0:T(1,128)} %add.51.s_ref), custom_call_target="tpu_custom_call" | custom-call | tf_op jit(solution)/shard_map/node_spectra/pallas_call | solution.py:326
  80.1 0.0 copy-start
  80.1 1.6 %copy-done = bf16[4,2,8,16,1024]{4,3,2,1,0:T(8,128)(2,1)S(1)} copy-done((bf16[4,2,8,16,1024]{4,3,2,1,0:T(8,128)(2,1)S(1)}, bf16[4,2,8,16,1024]{4,3,2,1,0:T(8,128)(2,1)}, u32[]{:S(2)}) %copy-start) | copy-done | bytes 2097176
  81.7 6.1 %load_series.1 = bf16[4,1024,1024]{2,1,0:T(8,128)(2,1)} custom-call(bf16[1024,256]{1,0:T(8,128)(2,1)S(1)} %pad_maximum_fusion.basis_ref, bf16[4,256,1024]{2,1,0:T(8,128)(2,1)S(1)} %bitcast.14), custom_call_target="tpu_custom_call" | custom-call | tf_op jit(solution)/shard_map/load_series/pallas_call | solution.py:358
  (2 shorter events, 0.0 us)
Async XLA Ops:
  80.1 1.6 %copy-start = (bf16[4,2,8,16,1024]{4,3,2,1,0:T(8,128)(2,1)S(1)}, bf16[4,2,8,16,1024]{4,3,2,1,0:T(8,128)(2,1)}, u32[]{:S(2)}) copy-start(bf16[4,2,8,16,1024]{4,3,2,1,0:T(8,128)(2,1)} %node_spectra.1) | copy-start | bytes 6291460
